TPU v7x, 512 devices: a whole 4x4x16 slice. The times are simulated.
512 devices in a mesh: sub: 8 (over y, z_hi), row: 8 (over z_lo), col: 8 (over x, core).
Axes of the slice: x: 4, y: 4, z: 16 (z_hi: 2, z_lo: 8; z = z_hi * 8 + z_lo), core: 2. Of those that a mesh axis runs over, the one named last changes fastest.
Arguments:
- root_inverse: float32 [8192, 8192], P(('sub', 'row'), 'col')
- panel: float32 [8192, 2048], P(('sub', 'row'), 'col'), may hold values from -0.125 to 0.125
- pattern: int32 [64, 16], P(('sub', 'row'), 'col'), may hold values from 0 to 1, as said below
- diag_inverse: float32 [2048, 2048], P(('sub', 'row'), 'col')
Outputs:
- off_block: float32 [8192, 2048], P(('sub', 'row'), 'col')
- diag_block: float32 [2048, 2048], P(('sub', 'row'), 'col')
Inputs may be any that keep to these rules, and one draw needn't show every extreme that they name: `pattern`: in every tile row, each aligned group of 2 tile columns (those of one index of col) has exactly one tile marked 1.
All inputs are finite; a program needn't handle non-finite values.
Results may differ from a plain program's by a relative error of at most 0.000078.
Values sent between devices are 32-bit elements; how exact they have to be, the bound alone decides.
A program may use at most 64 MiB of HBM per device.

v0:
```python
import jax
import jax.numpy as jnp
from jax import lax
from jax.sharding import PartitionSpec as P

highest = lax.Precision.HIGHEST


def rows_of_inverse(root_inverse):
    return lax.all_gather(root_inverse, "col", axis=1, tiled=True)


def local(root_inverse, panel, pattern, diag_inverse):
    tile_rows = panel.shape[0]
    marked = pattern[0].astype(jnp.float32)
    column_mask = jnp.repeat(marked, tile_rows)
    masked_panel = panel * column_mask[None, :]
    inverse_full = rows_of_inverse(root_inverse)
    accumulated = jnp.dot(
        inverse_full,
        lax.all_gather(masked_panel, ("sub", "row"), axis=0, tiled=True),
        precision=highest,
        preferred_element_type=jnp.float32,
    )
    off_block = -(accumulated * column_mask[None, :])
    panel_full_row = lax.all_gather(masked_panel, "col", axis=1, tiled=True)
    contribution = lax.dot_general(
        panel_full_row,
        off_block,
        (((0,), (0,)), ((), ())),
        precision=highest,
        preferred_element_type=jnp.float32,
    )
    update = lax.psum_scatter(contribution, ("sub", "row"), scatter_dimension=0, tiled=True)
    diag_block = diag_inverse - update
    return (off_block, diag_block)


def solution(mesh):
    in_specs = (
        P(("sub", "row"), "col"),
        P(("sub", "row"), "col"),
        P(("sub", "row"), "col"),
        P(("sub", "row"), "col"),
    )
    out_specs = (P(("sub", "row"), "col"), P(("sub", "row"), "col"))
    return jax.shard_map(local, mesh=mesh, in_specs=in_specs, out_specs=out_specs, check_vma=False)
```

profile of v0, /device:TPU:2, one launch (start us, length us, event | category | flops | bytes accessed | tf_op | source)
XLA Modules:
  0.0 950.3 jit_solution(14879854118065150119)
XLA Ops:
  7.2 0.0 all-gather.6.cloned.1.call-start
  7.2 0.7 all-gather.6.cloned.1.call-update
  7.9 0.0 all-gather.4.cloned.1.call-start
  7.9 0.7 convert_bitcast_fusion
  8.6 0.1 broadcast_bitcast_fusion
  8.7 1.6 broadcast_multiply_fusion
  10.2 0.0 all-gather.4.cloned.1.call-update
  10.3 0.0 all-gather.8.cloned.1.call-start
  10.3 0.7 all-gather.8.cloned.1.call-update
  11.0 0.0 reduce-scatter.2.cloned.1.call-start
  11.1 42.3 %all-gather.6.cloned.1.call-done = f32[128,8192]{1,0:T(8,128)} async-done(((f32[128,1024]{1,0:T(8,128)}), f32[128,8192]{1,0:T(8,128)}) %all-gather.6.cloned.1.call-update) | async-done | bytes 4194320 | tf_op jit(solution)/shard_map/all_gather | solution.py:10
  53.4 161.6 %all-gather.4.cloned.1.call-done = f32[8192,256]{1,0:T(8,128)} async-done(((f32[128,256]{1,0:T(8,128)}), f32[8192,256]{1,0:T(8,128)}) %all-gather.4.cloned.1.call-update) | async-done | bytes 8388624 | tf_op jit(solution)/shard_map/all_gather | solution.py:21
  215.0 16.3 %fusion = f32[256,128]{1,0:T(8,128)S(1)} fusion(f32[8192,256]{1,0:T(8,128)} %all-gather.4.cloned.1.call-done, f32[128,8192]{1,0:T(8,128)} %all-gather.6.cloned.1.call-done, f32[256]{0:T(256)S(1)} %broadcast_bitcast_fusion), kind=kOutput, calls=%fused_computation.1 | convolution fusion | flops 3221291008 | bytes 12715008 | tf_op jit(solution)/shard_map/dot_general | solution.py:19
  231.3 0.0 copy-start
  231.3 11.0 %all-gather.8.cloned.1.call-done = f32[128,2048]{1,0:T(8,128)} async-done(((f32[128,256]{1,0:T(8,128)}), f32[128,2048]{1,0:T(8,128)}) %all-gather.8.cloned.1.call-update) | async-done | bytes 1048592 | tf_op jit(solution)/shard_map/all_gather | solution.py:26
  242.3 4.4 fusion.1
  246.7 0.0 reduce-scatter.2.cloned.1.call-update
  246.7 0.8 copy.6
  247.5 694.9 %reduce-scatter.2.cloned.1.call-done = f32[32,256]{1,0:T(8,128)} async-done(((f32[2048,256]{1,0:T(8,128)}), f32[32,256]{1,0:T(8,128)}) %reduce-scatter.2.cloned.1.call-update) | async-done | bytes 32784 | tf_op jit(solution)/shard_map/reduce_scatter | solution.py:34
  942.4 0.0 copy-done
  942.4 1.4 sub.3
Async XLA Ops:
  7.2 46.2 %all-gather.6.cloned.1.call-start = ((), (), s32[]{:S(2)}) async-start(), calls=%async_computation.2 | async-start | bytes 4718592 | tf_op jit(solution)/shard_map/all_gather | solution.py:10
  7.9 207.1 %all-gather.4.cloned.1.call-start = ((), (), s32[]{:S(2)}) async-start(), calls=%async_computation.1 | async-start | bytes 8519680 | tf_op jit(solution)/shard_map/all_gather | solution.py:21
  10.3 232.0 %all-gather.8.cloned.1.call-start = ((), (), s32[]{:S(2)}) async-start(), calls=%async_computation.3 | async-start | bytes 1179648 | tf_op jit(solution)/shard_map/all_gather | solution.py:26
  11.0 931.4 %reduce-scatter.2.cloned.1.call-start = ((), (), s32[]{:S(2)}) async-start(), calls=%async_computation.4 | async-start | bytes 2129920 | tf_op jit(solution)/shard_map/reduce_scatter | solution.py:34
  231.3 711.1 %copy-start = (f32[32,256]{1,0:T(8,128)S(1)}, f32[32,256]{1,0:T(8,128)}, u32[]{:S(2)}) copy-start(f32[32,256]{1,0:T(8,128)} %param.7) | copy-start | bytes 98308
Sparse Core Ops, SparseCore 0:
  10.1 43.1 all-gather.5
  56.9 158.0 all-gather.3
  217.7 24.5 all-gather.7
  246.8 695.4 reduce-scatter.1
where the time goes:
time: 951 us; the launch traced here: 950 us
  waiting for transfers between devices  911 us (96%)
  matrix products  20.7 us (2%)
  between operations  13.8 us (1%)
    reduce_scatter x1, waiting for transfers between devices, local(): lax.psum_scatter(contribution, ('sub', 'row'), scatter_dimension=0, tiled...  695 us
    all_gather x1, waiting for transfers between devices, local(): lax.all_gather(masked_panel, ('sub', 'row'), axis=0, tiled=True)  162 us
    all_gather x1, waiting for transfers between devices, rows_of_inverse(): return lax.all_gather(root_inverse, 'col', axis=1, tiled=True)  42.3 us
  transfers between devices with their start and end apart: 4, of which 4 were waited for; matrix products, arithmetic and copies ran while one was open for 2% of the time, Pallas kernels for 0%

commit v1 on v0

--- a/solution.py
+++ b/solution.py
@@ -6,8 +6,13 @@
 highest = lax.Precision.HIGHEST
 
 
+def all_by_exchange(x, mesh_axis, along):
+    sent = jnp.stack([x] * lax.axis_size(mesh_axis))
+    return jnp.concatenate(lax.all_to_all(sent, mesh_axis, 0, 0), axis=along)
+
+
 def rows_of_inverse(root_inverse):
-    return lax.all_gather(root_inverse, "col", axis=1, tiled=True)
+    return all_by_exchange(root_inverse, "col", 1)
 
 
 def local(root_inverse, panel, pattern, diag_inverse):

time: 951 us -> 909 us (0.956)
  the two profiles are of different devices: /device:TPU:2 before, /device:TPU:4 now
where the time goes in v1:
time: 909 us; the launch traced here: 908 us
  waiting for transfers between devices  856 us (94%)
  matrix products  20.7 us (2%)
  between operations  13.8 us (2%)
  starting transfers between devices  10.5 us (1%)
    reduce_scatter x1, waiting for transfers between devices, local(): lax.psum_scatter(contribution, ('sub', 'row'), scatter_dimension=0, tiled...  695 us
    all_gather x1, waiting for transfers between devices, local(): lax.all_gather(masked_panel, ('sub', 'row'), axis=0, tiled=True)  103 us
    all_to_all x1, waiting for transfers between devices, all_by_exchange(): return jnp.concatenate(lax.all_to_all(sent, mesh_axis, 0, 0), axis=along)  45.8 us
  transfers between devices with their start and end apart: 4, of which 4 were waited for; matrix products, arithmetic and copies ran while one was open for 2% of the time, Pallas kernels for 0%

profile of v1, /device:TPU:4, one launch (start us, length us, event | category | flops | bytes accessed | tf_op | source)
XLA Modules:
  0.0 908.3 jit_solution(3263827340082395031)
XLA Ops:
  7.2 0.0 all-gather.3.cloned.1.call-start
  7.2 0.7 convert_bitcast_fusion
  7.9 0.1 broadcast_bitcast_fusion
  7.9 1.6 broadcast_multiply_fusion
  9.5 0.0 all-gather.3.cloned.1.call-update
  9.5 1.2 copy.7
  10.8 2.2 stack.2
  13.0 10.4 %all-to-all-start = ((f32[8,128,1024]{1,2,0:T(8,128)}), f32[8,128,1024]{1,2,0:T(8,128)}, u32[]{:S(2)}, u32[]{:S(2)}) async-start(f32[8,128,1024]{1,2,0:T(8,128)} %stack.2), calls=%async_computation | async-start | bytes 8388608 | tf_op jit(solution)/shard_map/all_to_all | solution.py:11
  23.4 0.0 all-gather.5.cloned.1.call-start
  23.4 0.7 all-gather.5.cloned.1.call-update
  24.1 0.0 reduce-scatter.2.cloned.1.call-start
  24.1 45.8 %all-to-all-done = f32[8,128,1024]{1,2,0:T(8,128)} async-done(((f32[8,128,1024]{1,2,0:T(8,128)}), f32[8,128,1024]{1,2,0:T(8,128)}, u32[]{:S(2)}, u32[]{:S(2)}) %all-to-all-start) | async-done | bytes 4194336 | tf_op jit(solution)/shard_map/all_to_all | solution.py:11
  69.9 102.9 %all-gather.3.cloned.1.call-done = f32[8192,256]{1,0:T(8,128)} async-done(((f32[128,256]{1,0:T(8,128)}), f32[8192,256]{1,0:T(8,128)}) %all-gather.3.cloned.1.call-update) | async-done | bytes 8388624 | tf_op jit(solution)/shard_map/all_gather | solution.py:26
  172.9 16.3 %fusion = f32[256,128]{1,0:T(8,128)S(1)} fusion(f32[8192,256]{1,0:T(8,128)} %all-gather.3.cloned.1.call-done, f32[128,8192]{0,1:T(8,128)} %bitcast.3, f32[256]{0:T(256)S(1)} %broadcast_bitcast_fusion), kind=kOutput, calls=%fused_computation.1 | convolution fusion | flops 3221291008 | bytes 12715008 | tf_op jit(solution)/shard_map/dot_general | solution.py:24
  189.2 0.0 copy-start
  189.2 11.3 %all-gather.5.cloned.1.call-done = f32[128,2048]{1,0:T(8,128)} async-done(((f32[128,256]{1,0:T(8,128)}), f32[128,2048]{1,0:T(8,128)}) %all-gather.5.cloned.1.call-update) | async-done | bytes 1048592 | tf_op jit(solution)/shard_map/all_gather | solution.py:31
  200.5 4.4 fusion.1
  204.9 0.0 reduce-scatter.2.cloned.1.call-update
  204.9 0.8 copy.8
  205.7 694.7 %reduce-scatter.2.cloned.1.call-done = f32[32,256]{1,0:T(8,128)} async-done(((f32[2048,256]{1,0:T(8,128)}), f32[32,256]{1,0:T(8,128)}) %reduce-scatter.2.cloned.1.call-update) | async-done | bytes 32784 | tf_op jit(solution)/shard_map/reduce_scatter | solution.py:39
  900.4 0.0 copy-done
  900.4 1.4 sub.3
Async XLA Ops:
  7.2 165.7 %all-gather.3.cloned.1.call-start = ((), (), s32[]{:S(2)}) async-start(), calls=%async_computation.2 | async-start | bytes 8519680 | tf_op jit(solution)/shard_map/all_gather | solution.py:26
  13.0 57.0 %all-to-all-start = ((f32[8,128,1024]{1,2,0:T(8,128)}), f32[8,128,1024]{1,2,0:T(8,128)}, u32[]{:S(2)}, u32[]{:S(2)}) async-start(f32[8,128,1024]{1,2,0:T(8,128)} %stack.2), calls=%async_computation | async-start | bytes 8388608 | tf_op jit(solution)/shard_map/all_to_all | solution.py:11
  23.4 177.1 %all-gather.5.cloned.1.call-start = ((), (), s32[]{:S(2)}) async-start(), calls=%async_computation.3 | async-start | bytes 1179648 | tf_op jit(solution)/shard_map/all_gather | solution.py:31
  24.1 876.3 %reduce-scatter.2.cloned.1.call-start = ((), (), s32[]{:S(2)}) async-start(), calls=%async_computation.4 | async-start | bytes 2129920 | tf_op jit(solution)/shard_map/reduce_scatter | solution.py:39
  189.2 711.2 %copy-start = (f32[32,256]{1,0:T(8,128)S(1)}, f32[32,256]{1,0:T(8,128)}, u32[]{:S(2)}) copy-start(f32[32,256]{1,0:T(8,128)} %param.7) | copy-start | bytes 98308
Sparse Core Ops, SparseCore 0:
  11.5 161.3 all-gather.2
  175.6 24.8 all-gather.4
  205.0 695.3 reduce-scatter.1
